TPU v7x, 512 devices: a whole 4x4x16 slice. The times are simulated.
512 devices in a mesh: feat: 32 (over x, y, core), dp: 16 (over z).
Axes of the slice: x: 4, y: 4, z: 16, core: 2. Of those that a mesh axis runs over, the one named last changes fastest.
Arguments:
- feature_table: bfloat16 [65536, 256], P('feat'), may hold values from -6 to 6
- row_state: float32 [65536], P('feat'), may hold values from 0.01 to 1
- rel_diag: bfloat16 [4096, 256], replicated, may hold values from -103 to 103
- slot_rows: int32 [512, 32, 128], P(('feat', 'dp')), may hold values from 0 to 2047
- slot_counts: int32 [512, 32], P(('feat', 'dp')), may hold values from 1 to 128, as said below
- head_bags: int32 [131072, 16], P(('feat', 'dp')), may hold values from 0 to 4095, as said below
- tail_bags: int32 [131072, 16], P(('feat', 'dp')), may hold values from 0 to 4095, as said below
- negative_bags: int32 [8192, 16], P(('feat', 'dp')), may hold values from 0 to 4095, as said below
- relation_ids: int32 [131072], P(('feat', 'dp')), may hold values from 0 to 4095
Outputs:
- triple_loss: float32 [131072], P(('feat', 'dp'))
- new_table: bfloat16 [65536, 256], P('feat')
- new_state: float32 [65536], P('feat')
Inputs may be any that keep to these rules, and one draw needn't show every extreme that they name: `slot_counts`: for every device some owner has exactly 128 live slots. `head_bags`: each entry o * 128 + c names a live slot of its device: c < slot_counts[d, o]. `tail_bags`: each entry o * 128 + c names a live slot of its device: c < slot_counts[d, o]. `negative_bags`: each entry o * 128 + c names a live slot of its device: c < slot_counts[d, o].
All inputs are finite; a program needn't handle non-finite values.
Results may differ from a plain program's by a relative error of at most 0.007.
Values may be sent and summed in bfloat16 or wider, within the bound.
No kernel may reach another device: no remote copies, remote signals or barrier semaphores. Data moves between devices by JAX's collectives and lax.ppermute only.
A program may use at most 64 MiB of HBM per device.

v0:
```python
import jax
import jax.numpy as jnp
from jax import lax
from jax.sharding import PartitionSpec as P

score_scale = 4.0
learn_rate = 0.1


def adagrad(table_part, state_part, gradient):
    fresh_state = state_part + jnp.mean(gradient * gradient, axis=1)
    updated = (
        table_part.astype(jnp.float32) - learn_rate * gradient / jnp.sqrt(fresh_state)[:, None]
    )
    return (updated.astype(jnp.bfloat16), fresh_state)


def on_device(
    feature_table,
    row_state,
    rel_diag,
    slot_rows,
    slot_counts,
    head_bags,
    tail_bags,
    negative_bags,
    relation_ids,
):
    n_feat = lax.axis_size("feat")
    cap = slot_rows.shape[2]
    width = feature_table.shape[1]
    local_rows = feature_table.shape[0]
    trip = head_bags.shape[0]
    slot_total = n_feat * cap
    asked = lax.all_to_all(slot_rows[0], "feat", split_axis=0, concat_axis=0, tiled=True)
    served = jnp.take(feature_table, asked.reshape(-1), axis=0).reshape(asked.shape + (width,))
    returned = lax.all_to_all(served, "feat", split_axis=0, concat_axis=0, tiled=True)
    fetched = returned
    live_mask = (
        lax.broadcasted_iota(jnp.int32, (n_feat, cap), 1) < slot_counts[0][:, None]
    ).reshape(slot_total)
    fetched = jnp.where(
        live_mask[:, None], fetched.reshape(slot_total, width), jnp.zeros((), jnp.bfloat16)
    )
    all_bags = jnp.concatenate([head_bags, tail_bags, negative_bags], axis=0)
    bag_size = all_bags.shape[1]
    pooled = jnp.sum(jnp.take(fetched, all_bags, axis=0), axis=1, dtype=jnp.float32)
    entity = (pooled / bag_size).astype(jnp.bfloat16)
    heads = entity[:trip]
    tails = entity[trip : 2 * trip]
    own_negs = entity[2 * trip :]
    negs = lax.all_gather(own_negs, "feat", axis=0, tiled=True)
    rel_pick = (
        relation_ids[:, None] == lax.broadcasted_iota(jnp.int32, (trip, rel_diag.shape[0]), 1)
    ).astype(jnp.bfloat16)
    scaling = jnp.dot(rel_pick, rel_diag, preferred_element_type=jnp.float32)
    tails_f = tails.astype(jnp.float32)
    query = (heads.astype(jnp.float32) * scaling).astype(jnp.bfloat16)
    query_f = query.astype(jnp.float32)
    positive = score_scale * jnp.sum(query_f * tails_f, axis=1)
    negative_score = score_scale * jnp.einsum(
        "td,nd->tn", query, negs, preferred_element_type=jnp.float32
    )
    highest = jnp.maximum(jnp.max(negative_score, axis=1), positive)
    total = jnp.exp(positive - highest) + jnp.sum(
        jnp.exp(negative_score - highest[:, None]), axis=1
    )
    log_total = highest + jnp.log(total)
    triple_loss = log_total - positive
    p_pos = jnp.exp(positive - log_total)
    p_neg = jnp.exp(negative_score - log_total[:, None]).astype(jnp.bfloat16)
    grad_query = score_scale * (
        (p_pos - 1.0)[:, None] * tails_f + jnp.dot(p_neg, negs, preferred_element_type=jnp.float32)
    )
    grad_head = grad_query * scaling
    grad_tail = score_scale * (p_pos - 1.0)[:, None] * query_f
    grad_negative = lax.psum_scatter(
        (
            score_scale * jnp.einsum("tn,td->nd", p_neg, query, preferred_element_type=jnp.float32)
        ).astype(jnp.bfloat16),
        "feat",
        scatter_dimension=0,
        tiled=True,
    ).astype(jnp.float32)
    entity_grad = jnp.concatenate([grad_head, grad_tail, grad_negative], axis=0) / bag_size
    slot_grad = (
        jnp.zeros((slot_total, width), jnp.float32)
        .at[all_bags]
        .add(jnp.broadcast_to(entity_grad[:, None, :], (entity_grad.shape[0], bag_size, width)))
    )
    slot_grad = (
        jnp.where(live_mask[:, None], slot_grad, jnp.zeros((), jnp.float32))
        .astype(jnp.bfloat16)
        .reshape(n_feat, cap, width)
    )
    owner_grads = lax.all_to_all(slot_grad, "feat", split_axis=0, concat_axis=0, tiled=True)
    partial_value = jax.ops.segment_sum(
        owner_grads.reshape(slot_total, width).astype(jnp.float32),
        asked.reshape(-1),
        num_segments=local_rows,
    )
    whole = lax.psum(partial_value.astype(jnp.bfloat16), "dp").astype(jnp.float32)
    new_table, new_state = adagrad(feature_table, row_state, whole)
    return (triple_loss, new_table, new_state)


def solution(mesh):
    in_specs = (
        P("feat", None),
        P("feat"),
        P(),
        P(("feat", "dp"), None, None),
        P(("feat", "dp"), None),
        P(("feat", "dp"), None),
        P(("feat", "dp"), None),
        P(("feat", "dp"), None),
        P(("feat", "dp")),
    )
    out_specs = (P(("feat", "dp")), P("feat", None), P("feat"))
    return jax.shard_map(
        on_device, mesh=mesh, in_specs=in_specs, out_specs=out_specs, check_vma=False
    )
```

profile of v0, /device:TPU:2, one launch (start us, length us, event | category | flops | bytes accessed | tf_op | source)
XLA Modules:
  0.0 496.0 jit_solution(13791528045355781160)
XLA Ops:
  7.2 15.7 %all_to_all.19 = s32[32,1,128]{2,1,0:T(1,128)S(1)} all-to-all(s32[32,1,128]{2,1,0:T(1,128)} %bitcast.38), channel_id=1, replica_groups=mesh['feat'=32,'dp'=16] {'feat'}, dimensions={0} | all-to-all | bytes 32768 | tf_op jit(solution)/shard_map/all_to_all | solution.py:35
  23.0 17.2 %gather_fusion = bf16[4096,256]{1,0:T(8,128)(2,1)} fusion(bf16[2048,256]{1,0:T(8,128)(2,1)} %param.9, s32[4096]{0:T(1024)S(1)} %broadcast_clamp_fusion), kind=kCustom, calls=%fused_computation | custom fusion | bytes 4210688 | tf_op jit(solution)/shard_map/jit(_take)/gather | solution.py:36
  40.2 2.9 broadcast_select_fusion
  43.1 5.9 %all-to-all-start.1 = ((bf16[32,128,256]{2,1,0:T(8,128)(2,1)}), bf16[32,128,256]{2,1,0:T(8,128)(2,1)}, u32[]{:S(2)}, u32[]{:S(2)}) async-start(bf16[32,128,256]{2,1,0:T(8,128)(2,1)} %broadcast_select_fusion), calls=%async_computation.1 | async-start | bytes 4194304 | tf_op jit(solution)/shard_map/all_to_all | solution.py:37
  49.9 25.2 %all-to-all-done.1 = bf16[32,128,256]{2,1,0:T(8,128)(2,1)} async-done(((bf16[32,128,256]{2,1,0:T(8,128)(2,1)}), bf16[32,128,256]{2,1,0:T(8,128)(2,1)}, u32[]{:S(2)}, u32[]{:S(2)}) %all-to-all-start.1) | async-done | bytes 2097184 | tf_op jit(solution)/shard_map/all_to_all | solution.py:37
  75.0 2.9 bitcast_select_fusion
  78.0 21.8 %gather_fusion.1 = bf16[8448,256]{1,0:T(8,128)(2,1)} fusion(bf16[4096,256]{1,0:T(8,128)(2,1)} %bitcast_select_fusion, s32[9216]{0:T(1024)S(1)} %pad_clamp_fusion), kind=kCustom, calls=%fused_computation.1 | custom fusion | bytes 8684544 | tf_op jit(solution)/shard_map/jit(_take)/gather | solution.py:47
  99.7 7.0 %convert_reduce_fusion = f32[528,256]{1,0:T(8,128)S(1)} fusion(bf16[528,16,256]{2,1,0:T(8,128)(2,1)} %bitcast.27, pred[528,16]{1,0:T(8,128)(4,1)S(1)} %copy.20), kind=kLoop, calls=%fused_computation.4 | loop fusion | flops 6352896 | bytes 4874496 | tf_op jit(solution)/shard_map/reduce_sum | solution.py:47
  106.8 25.0 %all_gather.3 = bf16[512,256]{1,0:T(8,128)(2,1)S(1)} all-gather(bf16[16,256]{1,0:T(8,128)(2,1)S(1)} %slice.17), channel_id=1, replica_groups=mesh['feat'=32,'dp'=16] {'feat'}, dimensions={0}, use_global_device_ids=true | all-gather | bytes 270336 | tf_op jit(solution)/shard_map/all_gather | solution.py:52
  131.8 1.5 fusion.14
  134.5 1.1 fusion.10
  135.7 1.3 fusion.12
  137.0 98.8 %reduce-scatter.2.cloned.1.call-done = bf16[16,256]{1,0:T(8,128)(2,1)} async-done(((bf16[512,256]{1,0:T(8,128)(2,1)}), bf16[16,256]{1,0:T(8,128)(2,1)}) %reduce-scatter.2.cloned.1.call-update) | async-done | bytes 8208 | tf_op jit(solution)/shard_map/reduce_scatter | solution.py:77
  235.9 0.7 convert_element_type.58
  236.6 4.0 broadcast_in_dim.67
  240.6 45.2 %scatter_custom_fusion = f32[4096,256]{1,0:T(8,128)} fusion(s32[8448]{0:T(1024)} %copy-done.3, f32[8448,256]{1,0:T(8,128)} %bitcast.28, f32[]{:T(128)} %constant.29.clone.1), kind=kCustom, calls=%fused_computation.17 | custom fusion | flops 2162688 | bytes 4194816 | tf_op jit(solution)/shard_map/scatter-add | solution.py:89
  285.8 2.6 select_convert_fusion
  288.4 31.4 %all_to_all.20 = bf16[32,128,256]{2,1,0:T(8,128)(2,1)} all-to-all(bf16[32,128,256]{2,1,0:T(8,128)(2,1)S(1)} %bitcast.30), channel_id=1, replica_groups=mesh['feat'=32,'dp'=16] {'feat'}, dimensions={0} | all-to-all | bytes 4194304 | tf_op jit(solution)/shard_map/all_to_all | solution.py:96
  319.9 22.3 %scatter_custom_fusion.1 = f32[2048,256]{1,0:T(8,128)} fusion(s32[4096]{0:T(1024)S(1)} %bitcast.33, bf16[4096,256]{1,0:T(8,128)(2,1)} %bitcast.29, f32[]{:T(128)} %constant.29.clone.1), kind=kCustom, calls=%fused_computation.5 | custom fusion | flops 2097152 | bytes 4194308 | tf_op jit(solution)/shard_map/scatter-add | solution.py:97
  342.1 2.8 convert_element_type.62
  345.5 138.8 %all-reduce.2.cloned.1.call-done = bf16[2048,256]{1,0:T(8,128)(2,1)} async-done(((bf16[2048,256]{1,0:T(8,128)(2,1)}), bf16[2048,256]{1,0:T(8,128)(2,1)}) %all-reduce.2.cloned.1.call-update) | async-done | bytes 1048592 | tf_op jit(solution)/shard_map/psum | solution.py:102
  484.3 1.6 fusion.6
  485.8 0.6 fusion.18
  486.4 2.7 fusion.5
  (57 shorter events, 2.8 us)
Async XLA Ops:
  7.2 124.7 %copy-start = (bf16[4096,256]{1,0:T(8,128)(2,1)S(1)}, bf16[4096,256]{1,0:T(8,128)(2,1)}, u32[]{:S(2)}) copy-start(bf16[4096,256]{1,0:T(8,128)(2,1)} %param.11) | copy-start | bytes 6291460
  43.1 6.0 %copy-start.8 = (s32[16,16]{1,0:T(8,128)S(1)}, s32[16,16]{1,0:T(8,128)}, u32[]{:S(2)}) copy-start(s32[16,16]{1,0:T(8,128)} %param.16) | copy-start | bytes 3076
  43.1 6.2 %copy-start.4 = (s32[256,16]{0,1:T(8,128)S(1)}, s32[256,16]{0,1:T(8,128)}, u32[]{:S(2)}) copy-start(s32[256,16]{0,1:T(8,128)} %param.15) | copy-start | bytes 49156
  43.1 6.2 %copy-start.5 = (s32[256,16]{0,1:T(8,128)S(1)}, s32[256,16]{0,1:T(8,128)}, u32[]{:S(2)}) copy-start(s32[256,16]{0,1:T(8,128)} %param.14) | copy-start | bytes 49156
  43.1 6.7 %copy-start.14 = (s32[1,32]{1,0:T(1,128)S(1)}, s32[1,32]{1,0:T(1,128)}, u32[]{:S(2)}) copy-start(s32[1,32]{1,0:T(1,128)} %param.13) | copy-start | bytes 388
  43.1 31.9 %all-to-all-start.1 = ((bf16[32,128,256]{2,1,0:T(8,128)(2,1)}), bf16[32,128,256]{2,1,0:T(8,128)(2,1)}, u32[]{:S(2)}, u32[]{:S(2)}) async-start(bf16[32,128,256]{2,1,0:T(8,128)(2,1)} %broadcast_select_fusion), calls=%async_computation.1 | async-start | bytes 4194304 | tf_op jit(solution)/shard_map/all_to_all | solution.py:37
  49.0 186.8 %reduce-scatter.2.cloned.1.call-start = ((), (), s32[]{:S(2)}) async-start(), calls=%async_computation.4 | async-start | bytes 270336 | tf_op jit(solution)/shard_map/reduce_scatter | solution.py:77
  49.7 28.2 %copy-start.3 = (s32[8448]{0:T(1024)}, s32[8448]{0:T(1024)S(1)}, u32[]{:S(2)}) copy-start(s32[8448]{0:T(1024)S(1)} %reshape.288) | copy-start | bytes 101380
  49.8 28.1 %copy-start.6 = (pred[4096]{0:T(1024)(128)(4,1)}, pred[4096]{0:T(1024)(128)(4,1)S(1)}, u32[]{:S(2)}) copy-start(pred[4096]{0:T(1024)(128)(4,1)S(1)} %fusion.15) | copy-start | bytes 12292
  99.7 32.1 %copy-start.15 = (s32[256]{0:T(256)S(1)}, s32[256]{0:T(256)}, u32[]{:S(2)}) copy-start(s32[256]{0:T(256)} %param.17) | copy-start | bytes 3076
  106.8 26.5 %copy-start.2 = (bf16[528,256]{1,0:T(8,128)(2,1)}, bf16[528,256]{1,0:T(8,128)(2,1)S(1)}, u32[]{:S(2)}) copy-start(bf16[528,256]{1,0:T(8,128)(2,1)S(1)} %multiply_convert_fusion) | copy-start | bytes 811012
  133.3 2.3 copy-start.11
  134.5 1.2 copy-start.9
  135.6 348.7 %all-reduce.2.cloned.1.call-start = ((), (), s32[]{:S(2)}) async-start(), calls=%async_computation.5 | async-start | bytes 2097152 | tf_op jit(solution)/shard_map/psum | solution.py:102
  240.6 45.2 %copy-start.7 = (pred[4096]{0:T(1024)(128)(4,1)S(1)}, pred[4096]{0:T(1024)(128)(4,1)}, u32[]{:S(2)}) copy-start(pred[4096]{0:T(1024)(128)(4,1)} %copy-done.6) | copy-start | bytes 12292
  342.1 2.8 copy-start.10
  342.1 2.8 copy-start.12
  342.1 143.7 %copy-start.13 = (f32[2048]{0:T(1024)S(1)}, f32[2048]{0:T(1024)}, u32[]{:S(2)}) copy-start(f32[2048]{0:T(1024)} %param.10) | copy-start | bytes 24580
  342.1 144.3 %copy-start.1 = (bf16[2048,256]{1,0:T(8,128)(2,1)S(1)}, bf16[2048,256]{1,0:T(8,128)(2,1)}, u32[]{:S(2)}) copy-start(bf16[2048,256]{1,0:T(8,128)(2,1)} %param.9) | copy-start | bytes 3145732
Sparse Core Ops, SparseCore 0:
  135.7 100.1 reduce-scatter.1
  345.0 139.1 all-reduce.1
where the time goes:
time: 497 us; the launch traced here: 496 us
  waiting for transfers between devices  263 us (53%)
  other arithmetic  92.9 us (19%)
  blocking collectives  72.2 us (15%)
  local copies, waits for them, and re-layouts  43.6 us (9%)
  between operations  14.3 us (3%)
  starting transfers between devices  6.02 us (1%)
    psum x1, waiting for transfers between devices, on_device(): lax.psum(partial_value.astype(jnp.bfloat16), 'dp').astype(jnp.float32)  139 us
    reduce_scatter x1, waiting for transfers between devices, on_device(): lax.psum_scatter((score_scale * jnp.einsum('tn,td->nd', p_neg, query, pre...  98.8 us
    scatter-add x1, other arithmetic, on_device(): slot_grad = jnp.zeros((slot_total, width), jnp.float32).at[all_bags].add(...  45.2 us
    all_to_all x1, blocking collectives, on_device(): lax.all_to_all(slot_grad, 'feat', split_axis=0, concat_axis=0, tiled=True)  31.4 us
    all_to_all x1, waiting for transfers between devices, on_device(): lax.all_to_all(served, 'feat', split_axis=0, concat_axis=0, tiled=True)  25.2 us
    all_gather x1, blocking collectives, on_device(): negs = lax.all_gather(own_negs, 'feat', axis=0, tiled=True)  25 us
    scatter-add x1, other arithmetic, on_device(): jax.ops.segment_sum(owner_grads.reshape(slot_total, width).astype(jnp.flo...  22.3 us
    gather x1, local copies, waits for them, and re-layouts, on_device(): jnp.take(fetched, all_bags, axis=0)  21.8 us
  transfers between devices with their start and end apart: 3, of which 3 were waited for; matrix products, arithmetic and copies ran while one was open for 1% of the time, Pallas kernels for 0%

commit v1 on v0

--- a/solution.py
+++ b/solution.py
@@ -1,3 +1,4 @@
+import functools
 import jax
 import jax.numpy as jnp
 from jax import lax
@@ -5,6 +6,14 @@
 
 score_scale = 4.0
 learn_rate = 0.1
+
+
+def goods_link(z, named_axis):
+    f_now = jax.lax.all_gather(z, named_axis)
+    return jnp.sum(f_now, axis=0)
+
+
+switch_yards = functools.partial(goods_link, named_axis="dp")
 
 
 def adagrad(table_part, state_part, gradient):
@@ -99,7 +108,7 @@
         asked.reshape(-1),
         num_segments=local_rows,
     )
-    whole = lax.psum(partial_value.astype(jnp.bfloat16), "dp").astype(jnp.float32)
+    whole = switch_yards(partial_value.astype(jnp.bfloat16)).astype(jnp.float32)
     new_table, new_state = adagrad(feature_table, row_state, whole)
     return (triple_loss, new_table, new_state)
 

time: 497 us -> 559 us (1.12)
  the two profiles are of different devices: /device:TPU:2 before, /device:TPU:1 now
where the time goes in v1:
time: 559 us; the launch traced here: 558 us
  waiting for transfers between devices  312 us (56%)
  other arithmetic  103 us (18%)
  blocking collectives  76.4 us (14%)
  local copies, waits for them, and re-layouts  43.6 us (8%)
  between operations  14.3 us (3%)
    all_gather x1, waiting for transfers between devices, goods_link(): f_now = jax.lax.all_gather(z, named_axis)  188 us
    reduce_scatter x1, waiting for transfers between devices, on_device(): lax.psum_scatter((score_scale * jnp.einsum('tn,td->nd', p_neg, query, pre...  96.4 us
    scatter-add x1, other arithmetic, on_device(): slot_grad = jnp.zeros((slot_total, width), jnp.float32).at[all_bags].add(...  45.2 us
    all_to_all x1, blocking collectives, on_device(): lax.all_to_all(slot_grad, 'feat', split_axis=0, concat_axis=0, tiled=True)  35.7 us
    all_to_all x1, waiting for transfers between devices, on_device(): lax.all_to_all(served, 'feat', split_axis=0, concat_axis=0, tiled=True)  27.6 us
    all_gather x1, blocking collectives, on_device(): negs = lax.all_gather(own_negs, 'feat', axis=0, tiled=True)  23.2 us
    scatter-add x1, other arithmetic, on_device(): jax.ops.segment_sum(owner_grads.reshape(slot_total, width).astype(jnp.flo...  22.3 us
    gather x1, local copies, waits for them, and re-layouts, on_device(): jnp.take(fetched, all_bags, axis=0)  21.8 us
  transfers between devices with their start and end apart: 3, of which 3 were waited for; matrix products, arithmetic and copies ran while one was open for 0% of the time, Pallas kernels for 0%

profile of v1, /device:TPU:1, one launch (start us, length us, event | category | flops | bytes accessed | tf_op | source)
XLA Modules:
  0.0 558.0 jit_solution(245534236201397288)
XLA Ops:
  7.2 17.5 %all_to_all.19 = s32[32,1,128]{2,1,0:T(1,128)S(1)} all-to-all(s32[32,1,128]{2,1,0:T(1,128)} %bitcast.40), channel_id=1, replica_groups=mesh['feat'=32,'dp'=16] {'feat'}, dimensions={0} | all-to-all | bytes 32768 | tf_op jit(solution)/shard_map/all_to_all | solution.py:44
  24.7 17.2 %gather_fusion = bf16[4096,256]{1,0:T(8,128)(2,1)} fusion(bf16[2048,256]{1,0:T(8,128)(2,1)} %param.9, s32[4096]{0:T(1024)S(1)} %broadcast_clamp_fusion), kind=kCustom, calls=%fused_computation | custom fusion | bytes 4210688 | tf_op jit(solution)/shard_map/jit(_take)/gather | solution.py:45
  41.9 2.9 broadcast_select_fusion
  44.8 5.1 all-to-all-start.1
  50.8 27.6 %all-to-all-done.1 = bf16[32,128,256]{2,1,0:T(8,128)(2,1)} async-done(((bf16[32,128,256]{2,1,0:T(8,128)(2,1)}), bf16[32,128,256]{2,1,0:T(8,128)(2,1)}, u32[]{:S(2)}, u32[]{:S(2)}) %all-to-all-start.1) | async-done | bytes 2097184 | tf_op jit(solution)/shard_map/all_to_all | solution.py:46
  78.4 2.9 bitcast_select_fusion
  81.3 21.8 %gather_fusion.1 = bf16[8448,256]{1,0:T(8,128)(2,1)} fusion(bf16[4096,256]{1,0:T(8,128)(2,1)} %bitcast_select_fusion, s32[9216]{0:T(1024)S(1)} %pad_clamp_fusion), kind=kCustom, calls=%fused_computation.1 | custom fusion | bytes 8684544 | tf_op jit(solution)/shard_map/jit(_take)/gather | solution.py:56
  103.1 7.0 %convert_reduce_fusion = f32[528,256]{1,0:T(8,128)S(1)} fusion(bf16[528,16,256]{2,1,0:T(8,128)(2,1)} %bitcast.28, pred[528,16]{1,0:T(8,128)(4,1)S(1)} %copy.24), kind=kLoop, calls=%fused_computation.4 | loop fusion | flops 6352896 | bytes 4874496 | tf_op jit(solution)/shard_map/reduce_sum | solution.py:56
  110.2 23.2 %all_gather.9 = bf16[512,256]{1,0:T(8,128)(2,1)S(1)} all-gather(bf16[16,256]{1,0:T(8,128)(2,1)S(1)} %slice.17), channel_id=1, replica_groups=mesh['feat'=32,'dp'=16] {'feat'}, dimensions={0}, use_global_device_ids=true | all-gather | bytes 270336 | tf_op jit(solution)/shard_map/all_gather | solution.py:61
  133.4 1.5 fusion.14
  136.0 1.1 fusion.10
  137.3 1.3 fusion.12
  138.6 96.4 %reduce-scatter.2.cloned.1.call-done = bf16[16,256]{1,0:T(8,128)(2,1)} async-done(((bf16[512,256]{1,0:T(8,128)(2,1)}), bf16[16,256]{1,0:T(8,128)(2,1)}) %reduce-scatter.2.cloned.1.call-update) | async-done | bytes 8208 | tf_op jit(solution)/shard_map/reduce_scatter | solution.py:86
  235.0 0.7 convert_element_type.60
  235.8 4.0 broadcast_in_dim.67
  239.8 45.2 %scatter_custom_fusion = f32[4096,256]{1,0:T(8,128)} fusion(s32[8448]{0:T(1024)} %copy-done.3, f32[8448,256]{1,0:T(8,128)} %bitcast.30, f32[]{:T(128)} %constant.30.clone.1), kind=kCustom, calls=%fused_computation.17 | custom fusion | flops 2162688 | bytes 4194816 | tf_op jit(solution)/shard_map/scatter-add | solution.py:98
  285.0 2.6 select_convert_fusion
  287.6 35.7 %all_to_all.20 = bf16[32,128,256]{2,1,0:T(8,128)(2,1)} all-to-all(bf16[32,128,256]{2,1,0:T(8,128)(2,1)S(1)} %bitcast.32), channel_id=1, replica_groups=mesh['feat'=32,'dp'=16] {'feat'}, dimensions={0} | all-to-all | bytes 4194304 | tf_op jit(solution)/shard_map/all_to_all | solution.py:105
  323.3 22.3 %scatter_custom_fusion.1 = f32[2048,256]{1,0:T(8,128)} fusion(s32[4096]{0:T(1024)S(1)} %bitcast.35, bf16[4096,256]{1,0:T(8,128)(2,1)} %bitcast.31, f32[]{:T(128)} %constant.30.clone.1), kind=kCustom, calls=%fused_computation.5 | custom fusion | flops 2097152 | bytes 4194308 | tf_op jit(solution)/shard_map/scatter-add | solution.py:106
  345.6 2.7 convert_element_type.64
  348.8 187.5 %all-gather.3.cloned.1.call-done = bf16[32768,256]{1,0:T(8,128)(2,1)} async-done(((bf16[2048,256]{1,0:T(8,128)(2,1)}), bf16[32768,256]{1,0:T(8,128)(2,1)}) %all-gather.3.cloned.1.call-update) | async-done | bytes 16777232 | tf_op jit(solution)/shard_map/all_gather | solution.py:12
  536.4 9.9 %reduce_sum.51 = bf16[2048,256]{1,0:T(8,128)(2,1)} reduce(bf16[16,2048,256]{2,1,0:T(8,128)(2,1)} %bitcast.29, bf16[]{:T(256)} %constant.29.clone.1), dimensions={0}, to_apply=%region_7.8 | reduce | flops 7864320 | bytes 17825794 | tf_op jit(solution)/shard_map/reduce_sum | solution.py:13
  546.3 1.6 fusion.6
  548.5 2.7 fusion.5
  (58 shorter events, 3.4 us)
Async XLA Ops:
  7.2 126.2 %copy-start = (bf16[4096,256]{1,0:T(8,128)(2,1)S(1)}, bf16[4096,256]{1,0:T(8,128)(2,1)}, u32[]{:S(2)}) copy-start(bf16[4096,256]{1,0:T(8,128)(2,1)} %param.11) | copy-start | bytes 6291460
  44.8 5.2 copy-start.8
  44.8 5.4 copy-start.4
  44.8 5.4 copy-start.5
  44.8 5.9 %copy-start.14 = (s32[1,32]{1,0:T(1,128)S(1)}, s32[1,32]{1,0:T(1,128)}, u32[]{:S(2)}) copy-start(s32[1,32]{1,0:T(1,128)} %param.13) | copy-start | bytes 388
  44.8 33.6 %all-to-all-start.1 = ((bf16[32,128,256]{2,1,0:T(8,128)(2,1)}), bf16[32,128,256]{2,1,0:T(8,128)(2,1)}, u32[]{:S(2)}, u32[]{:S(2)}) async-start(bf16[32,128,256]{2,1,0:T(8,128)(2,1)} %broadcast_select_fusion), calls=%async_computation.1 | async-start | bytes 4194304 | tf_op jit(solution)/shard_map/all_to_all | solution.py:46
  50.0 185.1 %reduce-scatter.2.cloned.1.call-start = ((), (), s32[]{:S(2)}) async-start(), calls=%async_computation.4 | async-start | bytes 270336 | tf_op jit(solution)/shard_map/reduce_scatter | solution.py:86
  50.7 30.6 %copy-start.3 = (s32[8448]{0:T(1024)}, s32[8448]{0:T(1024)S(1)}, u32[]{:S(2)}) copy-start(s32[8448]{0:T(1024)S(1)} %reshape.288) | copy-start | bytes 101380
  50.8 30.6 %copy-start.6 = (pred[4096]{0:T(1024)(128)(4,1)}, pred[4096]{0:T(1024)(128)(4,1)S(1)}, u32[]{:S(2)}) copy-start(pred[4096]{0:T(1024)(128)(4,1)S(1)} %fusion.15) | copy-start | bytes 12292
  103.1 30.3 %copy-start.15 = (s32[256]{0:T(256)S(1)}, s32[256]{0:T(256)}, u32[]{:S(2)}) copy-start(s32[256]{0:T(256)} %param.17) | copy-start | bytes 3076
  110.2 24.7 %copy-start.2 = (bf16[528,256]{1,0:T(8,128)(2,1)}, bf16[528,256]{1,0:T(8,128)(2,1)S(1)}, u32[]{:S(2)}) copy-start(bf16[528,256]{1,0:T(8,128)(2,1)S(1)} %multiply_convert_fusion) | copy-start | bytes 811012
  134.8 2.3 copy-start.11
  136.0 1.2 copy-start.9
  137.1 399.2 %all-gather.3.cloned.1.call-start = ((), (), s32[]{:S(2)}) async-start(), calls=%async_computation.5 | async-start | bytes 17825792 | tf_op jit(solution)/shard_map/all_gather | solution.py:12
  239.8 45.2 %copy-start.7 = (pred[4096]{0:T(1024)(128)(4,1)S(1)}, pred[4096]{0:T(1024)(128)(4,1)}, u32[]{:S(2)}) copy-start(pred[4096]{0:T(1024)(128)(4,1)} %copy-done.6) | copy-start | bytes 12292
  345.6 2.7 copy-start.10
  345.6 2.7 copy-start.12
  536.4 11.5 %copy-start.13 = (f32[2048]{0:T(1024)S(1)}, f32[2048]{0:T(1024)}, u32[]{:S(2)}) copy-start(f32[2048]{0:T(1024)} %param.10) | copy-start | bytes 24580
  536.4 12.1 %copy-start.1 = (bf16[2048,256]{1,0:T(8,128)(2,1)S(1)}, bf16[2048,256]{1,0:T(8,128)(2,1)}, u32[]{:S(2)}) copy-start(bf16[2048,256]{1,0:T(8,128)(2,1)} %param.9) | copy-start | bytes 3145732
Sparse Core Ops, SparseCore 0:
  137.2 97.7 reduce-scatter.1
  348.4 187.9 all-gather.2
